TPU v7x, 256 devices: a whole 4x4x8 slice. The times are simulated.
256 devices in a mesh: pair: 64 (over z, y, core), rep: 4 (over x).
Axes of the slice: x: 4, y: 4, z: 8, core: 2. Of those that a mesh axis runs over, the one named last changes fastest.
Arguments:
- tau_ao: bfloat16 [4096, 65536], P('pair'), may hold values from -6 to 6
- slab_sizes: int32 [256], replicated, may hold values from 1 to 512, 65536 in all
- integrals: bfloat16 [256, 512, 1024], P('pair', 'rep'), may hold values from -0.0234375 to 0.0234375
- transform: float32 [1024, 512], replicated, may hold values from -0.1875 to 0.1875
Outputs:
- ladder_mo: float32 [4096, 512], P('pair', 'rep')
Inputs may be any that keep to these rules, and one draw needn't show every extreme that they name: `slab_sizes`: the sizes sum to 65536 and the largest equals 512.
All inputs are finite; a program needn't handle non-finite values.
Results may differ from a plain program's by a relative error of at most 0.0003.
Values may be sent and summed in bfloat16 or wider, within the bound.
No kernel may reach another device: no remote copies, remote signals or barrier semaphores. Data moves between devices by JAX's collectives and lax.ppermute only.
A program may use at most 128 MiB of HBM per device.

v0:
```python
import jax
import jax.numpy as jnp
from jax import lax
from jax.sharding import PartitionSpec as P


def pick_columns(tau_rows, offsets, sizes_int, slot_index):
    packed_cols = tau_rows.shape[1]
    columns = jnp.clip(offsets[:, None] + slot_index[None, :], 0, packed_cols - 1)
    filled = (slot_index[None, :] < sizes_int[:, None]).reshape(-1)
    picked = jnp.take(tau_rows, columns.reshape(-1), axis=1)
    return jnp.where(filled[None, :], picked, jnp.zeros_like(picked))


def regroup(picked, pair_count, width):
    outgoing = picked.reshape(picked.shape[0], pair_count, width)
    arrived = lax.all_to_all(outgoing, "pair", split_axis=1, concat_axis=0, tiled=True)
    return arrived.reshape(pair_count * picked.shape[0], width)


def contract(pair_amps, slab_weights, transform):
    partial_ao = lax.psum_scatter(
        jnp.dot(pair_amps, slab_weights, preferred_element_type=jnp.float32),
        "pair",
        scatter_dimension=0,
        tiled=True,
    )
    return jnp.dot(partial_ao, transform, precision=lax.Precision.HIGHEST)


def body(tau_ao, slab_sizes, integrals, transform):
    pair_count = lax.axis_size("pair")
    rep_index = lax.axis_index("rep")
    slabs_here, slab_rows, out_width = integrals.shape
    offsets = jnp.cumsum(slab_sizes) - slab_sizes
    slot_index = rep_index * slab_rows + jnp.arange(slab_rows, dtype=jnp.int32)
    picked = pick_columns(tau_ao, offsets, slab_sizes, slot_index)
    pair_amps = regroup(picked, pair_count, slabs_here * slab_rows)
    slab_weights = integrals.reshape(slabs_here * slab_rows, out_width)
    forward = contract(pair_amps, slab_weights, transform)
    return lax.psum_scatter(forward, "rep", scatter_dimension=1, tiled=True)


def solution(mesh):
    return jax.shard_map(
        body,
        mesh=mesh,
        in_specs=(P("pair", None), P(), P("pair", "rep", None), P()),
        out_specs=P("pair", "rep"),
        check_vma=False,
    )
```

profile of v0, /device:TPU:1, one launch (start us, length us, event | category | flops | bytes accessed | tf_op | source)
XLA Modules:
  0.0 486.5 jit_solution(8310704746095908760)
XLA Ops:
  6.5 0.0 copy-start
  6.5 0.0 reduce-scatter.3.cloned.1.call-start
  6.5 0.9 lt.48
  7.5 1.0 reduce-window.9
  8.5 0.1 slice.7
  8.6 0.1 slice_reduce_fusion
  8.7 0.8 bitcast_subtract_fusion
  9.4 0.1 add_clamp_fusion
  9.6 0.1 add.69
  9.7 15.6 %copy.6 = bf16[64,65536]{0,1:T(8,128)(2,1)} copy(bf16[64,65536]{1,0:T(8,128)(2,1)} %param.4) | data formatting | bytes 16777216 | tf_op args[0]
  25.2 0.1 compare_select_fusion
  25.4 117.3 %gather_fusion = bf16[32768,64]{1,0:T(8,128)(2,1)} fusion(bf16[64,65536]{0,1:T(8,128)(2,1)} %copy.6, s32[32768]{0:T(1024)S(1)} %broadcast_clamp_fusion), kind=kCustom, calls=%fused_computation | custom fusion | bytes 8519680 | tf_op jit(solution)/shard_map/jit(_take)/gather | solution.py:11
  142.7 8.6 %copy.7 = bf16[64,64,512]{2,0,1:T(8,128)(2,1)} copy(bf16[64,64,512]{0,2,1:T(8,128)(2,1)} %bitcast.32) | data formatting | bytes 8388608 | tf_op jit(solution)/shard_map/jit(_take)/gather | solution.py:11
  151.2 0.1 lt.49
  151.4 0.1 add.70
  151.5 0.1 bitcast_compare_fusion
  151.6 2.8 select_select_fusion
  154.4 0.0 copy-start.1
  154.4 107.7 %all_to_all.15 = bf16[64,64,512]{2,0,1:T(8,128)(2,1)S(1)} all-to-all(bf16[64,64,512]{2,0,1:T(8,128)(2,1)S(1)} %select_select_fusion), channel_id=1, replica_groups=mesh['pair'=64,'rep'=4] {'pair'}, dimensions={1} | all-to-all | bytes 8388608 | tf_op jit(solution)/shard_map/all_to_all | solution.py:17
  262.1 0.0 copy-done.1
  262.1 8.1 %fusion.1 = f32[4096,1024]{1,0:T(8,128)} fusion(bf16[4096,512]{1,0:T(8,128)(2,1)S(1)} %bitcast.33, bf16[512,1024]{1,0:T(8,128)(2,1)S(1)} %bitcast.39), kind=kOutput, calls=%fused_computation.14 | convolution fusion | flops 4294967296 | bytes 22020096 | tf_op jit(solution)/shard_map/dot_general | solution.py:23
  270.2 0.0 reduce-scatter.3.cloned.1.call-update
  270.2 0.0 reduce-scatter.5.cloned.1.call-start
  270.3 183.1 %reduce-scatter.3.cloned.1.call-done = f32[64,1024]{1,0:T(8,128)} async-done(((f32[4096,1024]{1,0:T(8,128)}), f32[64,1024]{1,0:T(8,128)}) %reduce-scatter.3.cloned.1.call-update) | async-done | bytes 262160 | tf_op jit(solution)/shard_map/reduce_scatter | solution.py:22
  453.4 0.0 copy-done
  453.4 3.0 fusion.2
  456.3 0.0 reduce-scatter.5.cloned.1.call-update
  456.4 23.3 %reduce-scatter.5.cloned.1.call-done = f32[64,128]{1,0:T(8,128)} async-done(((f32[64,512]{1,0:T(8,128)}), f32[64,128]{1,0:T(8,128)}) %reduce-scatter.5.cloned.1.call-update) | async-done | bytes 32784 | tf_op jit(solution)/shard_map/reduce_scatter | solution.py:41
  (4 shorter events, 0.1 us)
Async XLA Ops:
  6.5 446.8 %copy-start = (f32[1024,512]{1,0:T(8,128)S(1)}, f32[1024,512]{1,0:T(8,128)}, u32[]{:S(2)}) copy-start(f32[1024,512]{1,0:T(8,128)} %param.7) | copy-start | bytes 6291460
  6.5 446.8 %reduce-scatter.3.cloned.1.call-start = ((), (), s32[]{:S(2)}) async-start(), calls=%async_computation.3 | async-start | bytes 17039360 | tf_op jit(solution)/shard_map/reduce_scatter | solution.py:22
  154.4 107.7 %copy-start.1 = (bf16[4,128,1024]{2,1,0:T(8,128)(2,1)S(1)}, bf16[4,128,1024]{2,1,0:T(8,128)(2,1)}, u32[]{:S(2)}) copy-start(bf16[4,128,1024]{2,1,0:T(8,128)(2,1)} %param.6) | copy-start | bytes 3145732
  270.2 209.5 %reduce-scatter.5.cloned.1.call-start = ((), (), s32[]{:S(2)}) async-start(), calls=%async_computation.4 | async-start | bytes 163840 | tf_op jit(solution)/shard_map/reduce_scatter | solution.py:41
Sparse Core Ops, SparseCore 0:
  270.3 182.9 reduce-scatter.2
  456.5 23.1 reduce-scatter.4
where the time goes:
time: 489 us; the launch traced here: 487 us
  waiting for transfers between devices  206 us (42%)
  local copies, waits for them, and re-layouts  143 us (29%)
  blocking collectives  108 us (22%)
  between operations  13.5 us (3%)
  matrix products  11 us (2%)
  other arithmetic  4.91 us (1%)
    reduce_scatter x1, waiting for transfers between devices, contract(): lax.psum_scatter(jnp.dot(pair_amps, slab_weights, preferred_element_type=...  183 us
    gather x2, local copies, waits for them, and re-layouts, pick_columns(): picked = jnp.take(tau_rows, columns.reshape(-1), axis=1)  126 us
    all_to_all x1, blocking collectives, regroup(): lax.all_to_all(outgoing, 'pair', split_axis=1, concat_axis=0, tiled=True)  108 us
    reduce_scatter x1, waiting for transfers between devices, body(): return lax.psum_scatter(forward, 'rep', scatter_dimension=1, tiled=True)  23.3 us
    unnamed x5, local copies, waits for them, and re-layouts  15.6 us
  transfers between devices with their start and end apart: 2, of which 2 were waited for; matrix products, arithmetic and copies ran while one was open for 0% of the time, Pallas kernels for 0%

commit v1 on v0

v1 whole, which is shorter than its diff:
```python
import functools

import jax
import jax.numpy as jnp
from jax import lax
from jax.experimental import pallas as pl
from jax.experimental.pallas import tpu as pltpu
from jax.sharding import Mesh
from jax.sharding import PartitionSpec as P

LANES = 128
PAD = 16
VMEM = 56 * 1024 * 1024
SHIFTS = (64, 32, 16, 8, 4, 2, 1)
TOP = 8.0
FRACTION = 12


def power(exponent, sign):
    out = jnp.ones_like(exponent)
    for bit in SHIFTS:
        has = exponent >= bit
        out = jnp.where(has, out * (2.0 ** (sign * bit)), out)
        exponent = jnp.where(has, exponent - bit, exponent)
    return out


def split3(value):
    first = value.astype(jnp.bfloat16)
    rest = value - first.astype(jnp.float32)
    second = rest.astype(jnp.bfloat16)
    third = (rest - second.astype(jnp.float32)).astype(jnp.bfloat16)
    return first, second, third


def fold_kernel(slab_ref, transform_ref, out_ref):
    rows = slab_ref[...]
    terms = split3(transform_ref[...])
    folded = sum(jnp.dot(rows, t, preferred_element_type=jnp.float32) for t in reversed(terms))
    peak = jnp.max(jnp.abs(folded), axis=1, keepdims=True)
    exponent = jnp.zeros_like(peak)
    for bit in SHIFTS:
        fits = (peak * (2.0 ** bit) < TOP) & (exponent + bit <= 96)
        peak = jnp.where(fits, peak * (2.0 ** bit), peak)
        exponent = jnp.where(fits, exponent + bit, exponent)
    scaled = folded * power(exponent, 1) * (2.0 ** FRACTION)
    codes = jnp.clip(jnp.round(scaled), -32767.0, 32767.0)
    count = rows.shape[0]
    out_ref[:count] = codes.astype(jnp.int32).astype(jnp.int16)
    across = jnp.transpose(jnp.broadcast_to(exponent, (count, LANES)))
    out_ref[count:] = across[:PAD].astype(jnp.int32).astype(jnp.int16)


def fold(slabs, transform):
    rows, cols = slabs.shape[0], transform.shape[1]
    return pl.pallas_call(
        fold_kernel,
        out_shape=jax.ShapeDtypeStruct((rows + PAD, cols), jnp.int16),
        compiler_params=pltpu.CompilerParams(vmem_limit_bytes=VMEM),
        cost_estimate=pl.CostEstimate(flops=6 * rows * slabs.shape[1] * cols, bytes_accessed=4 << 20, transcendentals=0),
        name="fold",
    )(slabs, transform)


def pick_kernel(per_device, width, sizes_ref, rep_ref, tau_ref, out_ref, offset_ref):
    group, groups = pl.program_id(0), pl.num_programs(0)
    slabs = sizes_ref.shape[0]

    @pl.when(group == 0)
    def _():
        def step(s, total):
            offset_ref[s] = total
            return total + sizes_ref[s]

        lax.fori_loop(0, slabs, step, jnp.int32(0))

    start = rep_ref[0] * width
    last = tau_ref.shape[1] // LANES - 2
    lane = lax.broadcasted_iota(jnp.int32, (tau_ref.shape[0], LANES), 1)

    def one(n, carry):
        slab = (n // per_device * groups + group) * per_device + n % per_device
        base = offset_ref[slab] + start
        block = jnp.minimum(base // LANES, last)
        shift = jnp.minimum(base - block * LANES, 2 * LANES - 1)
        window = tau_ref[:, pl.ds(pl.multiple_of(block * LANES, LANES), 2 * LANES)].astype(jnp.float32)
        moved = pltpu.roll(window, 2 * LANES - shift, axis=1)[:, :LANES]
        kept = jnp.where(lane < sizes_ref[slab] - start, moved, 0.0)
        out_ref[0, :, pl.ds(pl.multiple_of(n * LANES, LANES), LANES)] = kept.astype(jnp.bfloat16)
        return carry

    lax.fori_loop(0, slabs // groups, one, 0)


def pick(tau, sizes, rep, groups, per_device, width):
    rows, cols = tau.shape[0], sizes.shape[0] // groups * width
    return pl.pallas_call(
        functools.partial(pick_kernel, per_device, width),
        grid_spec=pltpu.PrefetchScalarGridSpec(
            num_scalar_prefetch=2,
            grid=(groups,),
            in_specs=[pl.BlockSpec(tau.shape, lambda g, *_: (0, 0), pipeline_mode=pl.Buffered(1))],
            out_specs=pl.BlockSpec((1, rows, cols), lambda g, *_: (g, 0, 0)),
            scratch_shapes=[pltpu.SMEM((sizes.shape[0],), jnp.int32)],
        ),
        out_shape=jax.ShapeDtypeStruct((groups, rows, cols), jnp.bfloat16),
        compiler_params=pltpu.CompilerParams(vmem_limit_bytes=VMEM),
        cost_estimate=pl.CostEstimate(flops=0, bytes_accessed=12 << 20, transcendentals=0),
        name="pick",
    )(sizes, rep, tau)


def contract_kernel(amps_ref, coded_ref, out_ref):
    depth = amps_ref.shape[1]
    reps = out_ref.shape[1]

    @pl.when(pl.program_id(0) == 0)
    def _():
        out_ref[...] = jnp.zeros_like(out_ref)

    code = coded_ref[0, :depth].astype(jnp.int32).astype(jnp.float32)
    high = code.astype(jnp.bfloat16)
    low = (code - high.astype(jnp.float32)).astype(jnp.bfloat16)
    exponent = coded_ref[0, depth:].astype(jnp.int32).astype(jnp.float32)[:1]
    scale = power(exponent, -1) * (2.0 ** -FRACTION)
    amps = (amps_ref[...].astype(jnp.float32) * scale).astype(jnp.bfloat16)
    part = jnp.dot(amps, high, preferred_element_type=jnp.float32)
    part = part + jnp.dot(amps, low, preferred_element_type=jnp.float32)
    rows = out_ref.shape[2]
    for g in range(out_ref.shape[0]):
        for r in range(reps):
            out_ref[g, r] += part[g * rows:(g + 1) * rows, r * LANES:(r + 1) * LANES]


def contract(amps, coded, groups, reps):
    chunks, padded, cols = coded.shape
    depth = padded - PAD
    shape = (groups, reps, amps.shape[0] // groups, cols // reps)
    return pl.pallas_call(
        contract_kernel,
        grid=(chunks,),
        in_specs=[
            pl.BlockSpec((amps.shape[0], depth), lambda k: (0, k)),
            pl.BlockSpec((1, padded, cols), lambda k: (k, 0, 0)),
        ],
        out_specs=pl.BlockSpec(shape, lambda k: (0, 0, 0, 0)),
        out_shape=jax.ShapeDtypeStruct(shape, jnp.float32),
        compiler_params=pltpu.CompilerParams(vmem_limit_bytes=VMEM),
        cost_estimate=pl.CostEstimate(flops=4 * amps.size * cols, bytes_accessed=9 << 20, transcendentals=0),
        name="contract",
    )(amps, coded)


def body(tau_ao, slab_sizes, integrals, transform):
    groups = lax.axis_size("y") * lax.axis_size("core")
    reps = lax.axis_size("rep")
    per_device, width, depth = integrals.shape
    coded = fold(integrals.reshape(per_device * width, depth), transform)
    line = lax.all_gather(coded, "z", axis=0, tiled=False)
    rep = lax.axis_index("rep").reshape(1)
    picked = pick(tau_ao, slab_sizes, rep, groups, per_device, width)
    arrived = lax.all_to_all(picked, ("y", "core"), split_axis=0, concat_axis=0, tiled=True)
    amps = arrived.reshape(-1, arrived.shape[-1])
    partial = contract(amps, line, groups, reps)
    partial = partial.reshape(groups * reps, *partial.shape[2:])
    shares = lax.all_to_all(partial, ("y", "core", "rep"), split_axis=0, concat_axis=0, tiled=True)
    return jnp.sum(shares, axis=0)


def solution(mesh):
    fine = Mesh(mesh.devices.reshape(8, 4, 2, 4), ("z", "y", "core", "rep"))
    pair = ("z", "y", "core")
    return jax.shard_map(
        body,
        mesh=fine,
        in_specs=(P(pair, None), P(), P(pair, "rep", None), P()),
        out_specs=P(pair, "rep"),
        check_vma=False,
    )
```

time: 489 us -> 126 us (0.26)
  waiting for transfers between devices: 206 us -> 0.01 us
  local copies, waits for them, and re-layouts: 143 us -> 0 us
  Pallas kernels: 0 us -> 46.8 us
  blocking collectives: 108 us -> 70.8 us
  between operations: 13.5 us -> 0.01 us
  matrix products: 11 us -> 0 us
  starting transfers between devices: 0.04 us -> 7.67 us
    reduce_scatter x2 -> x0, waiting for transfers between devices: 206 us -> none  [the longest x1 183 us: contract(): lax.psum_scatter(jnp.dot(pair_amps, slab_weights, preferred_element_type=...]
    gather x2 -> x0, local copies, waits for them, and re-layouts: 126 us -> none  [pick_columns(): picked = jnp.take(tau_rows, columns.reshape(-1), axis=1)]
    all_to_all x1, blocking collectives: 108 us -> 23.9 us  [body(): lax.all_to_all(partial, ('y', 'core', 'rep'), split_axis=0, concat_axis=0...]
    all_gather x0 -> x1, blocking collectives: none -> 46.9 us  [body(): line = lax.all_gather(coded, 'z', axis=0, tiled=False)]
    pallas_call x0 -> x3, Pallas kernels: none -> 46.8 us  [the longest x1 31.2 us: pick(): pl.pallas_call(functools.partial(pick_kernel, per_device, width), grid_sp...]
    unnamed x5 -> x0, local copies, waits for them, and re-layouts: 15.6 us -> none
    dot_general x2 -> x0, matrix products: 11 us -> none  [the longest x1 8.07 us: contract(): jnp.dot(pair_amps, slab_weights, preferred_element_type=jnp.float32)]
    all_to_all x0 -> x1, starting transfers between devices: none -> 7.67 us  [body(): lax.all_to_all(picked, ('y', 'core'), split_axis=0, concat_axis=0, tiled=...]
  transfers between devices with their start and end apart: 2 -> 1, of which waited for: 2 -> 0; matrix products, arithmetic and copies ran while one was open for 0% -> 0% of each run, Pallas kernels for 0% -> 4%
where the time goes in v1:
time: 126 us
  blocking collectives  70.8 us (56%)
  Pallas kernels  46.8 us (37%)
  starting transfers between devices  7.67 us (6%)
    all_gather x1, blocking collectives, body(): line = lax.all_gather(coded, 'z', axis=0, tiled=False)  46.9 us
    pallas_call x1, Pallas kernels, pick(): pl.pallas_call(functools.partial(pick_kernel, per_device, width), grid_sp...  31.2 us
    all_to_all x1, blocking collectives, body(): lax.all_to_all(partial, ('y', 'core', 'rep'), split_axis=0, concat_axis=0...  23.9 us
    pallas_call x1, Pallas kernels, contract(): pl.pallas_call(contract_kernel, grid=(chunks,), in_specs=[pl.BlockSpec((a...  10.1 us
    all_to_all x1, starting transfers between devices, body(): lax.all_to_all(picked, ('y', 'core'), split_axis=0, concat_axis=0, tiled=...  7.67 us
    pallas_call x1, Pallas kernels, fold(): pl.pallas_call(fold_kernel, out_shape=jax.ShapeDtypeStruct((rows + PAD, c...  5.42 us
  transfers between devices with their start and end apart: 1, of which 0 were waited for; matrix products, arithmetic and copies ran while one was open for 0% of the time, Pallas kernels for 4%

profile of v1, /device:TPU:1, one launch (start us, length us, event | category | flops | bytes accessed | tf_op | source)
XLA Modules:
  0.0 125.9 jit_solution(12664860442573556733)
XLA Ops:
  0.0 31.2 %pick.1 = bf16[8,64,4096]{2,1,0:T(8,128)(2,1)} custom-call(s32[256]{0:T(256)} %sizes_ref.1, s32[1]{0:T(128)} %bitcast.rep_ref, bf16[64,65536]{1,0:T(8,128)(2,1)} %tau_ref.1), custom_call_target="tpu_custom_call" | custom-call | bytes 12582912 | tf_op jit(solution)/shard_map/pick/pallas_call | solution.py:97
  31.2 7.7 %all-to-all-start = ((bf16[8,64,4096]{2,1,0:T(8,128)(2,1)}), bf16[8,64,4096]{2,1,0:T(8,128)(2,1)}, u32[]{:S(2)}, u32[]{:S(2)}) async-start(bf16[8,64,4096]{2,1,0:T(8,128)(2,1)} %pick.1), calls=%async_computation | async-start | bytes 8388608 | tf_op jit(solution)/shard_map/all_to_all | solution.py:162
  38.9 5.4 %fold.1 = s16[528,512]{1,0:T(8,128)(2,1)} custom-call(bf16[512,1024]{1,0:T(8,128)(2,1)} %bitcast.7, f32[1024,512]{1,0:T(8,128)} %transform_ref.1), custom_call_target="tpu_custom_call" | custom-call | flops 1610612736 | bytes 4194304 | tf_op jit(solution)/shard_map/fold/pallas_call | solution.py:56
  44.3 46.9 %all-gather.2 = s16[4224,512]{1,0:T(8,128)(2,1)} all-gather(s16[528,512]{1,0:T(8,128)(2,1)} %fold.1), channel_id=2, replica_groups=mesh['z'=8,'y'=4,'core'=2,'rep'=4] {'z'}, dimensions={0}, use_global_device_ids=true | all-gather | bytes 4866048 | tf_op jit(solution)/shard_map/all_gather | solution.py:159
  91.2 0.0 all-to-all-done
  91.2 10.1 %contract.1 = f32[8,4,64,128]{3,2,1,0:T(8,128)} custom-call(bf16[512,4096]{1,0:T(8,128)(2,1)} %bitcast.1.amps_ref, s16[8,528,512]{2,1,0:T(8,128)(2,1)} %bitcast.5), custom_call_target="tpu_custom_call" | custom-call | flops 4294967296 | bytes 9437184 | tf_op jit(solution)/shard_map/contract/pallas_call | solution.py:139
  101.3 23.9 %all_to_all.10 = f32[32,64,128]{2,1,0:T(8,128)S(1)} all-to-all(f32[32,64,128]{2,1,0:T(8,128)} %bitcast.6), channel_id=1, replica_groups=mesh['z'=8,'y'=4,'core'=2,'rep'=4] {'y','core','rep'}, dimensions={0} | all-to-all | bytes 2097152 | tf_op jit(solution)/shard_map/all_to_all | solution.py:166
  125.2 0.7 reduce_sum.9
Async XLA Ops:
  31.2 60.0 %all-to-all-start = ((bf16[8,64,4096]{2,1,0:T(8,128)(2,1)}), bf16[8,64,4096]{2,1,0:T(8,128)(2,1)}, u32[]{:S(2)}, u32[]{:S(2)}) async-start(bf16[8,64,4096]{2,1,0:T(8,128)(2,1)} %pick.1), calls=%async_computation | async-start | bytes 8388608 | tf_op jit(solution)/shard_map/all_to_all | solution.py:162

commit v2 on v1

v2 whole, which is shorter than its diff:
```python
import functools

import jax
import jax.numpy as jnp
from jax import lax
from jax.experimental import pallas as pl
from jax.experimental.pallas import tpu as pltpu
from jax.sharding import Mesh
from jax.sharding import PartitionSpec as P

LANES = 128
PAD = 16
VMEM = 56 * 1024 * 1024
SHIFTS = (64, 32, 16, 8, 4, 2, 1)
TOP = 8.0
FRACTION = 12


def power(exponent, sign):
    out = jnp.ones_like(exponent)
    for bit in SHIFTS:
        has = exponent >= bit
        out = jnp.where(has, out * (2.0 ** (sign * bit)), out)
        exponent = jnp.where(has, exponent - bit, exponent)
    return out


def split2(value):
    first = value.astype(jnp.bfloat16)
    return first, (value - first.astype(jnp.float32)).astype(jnp.bfloat16)


def fold_kernel(slab_ref, transform_ref, out_ref):
    rows = slab_ref[...]
    high, low = split2(transform_ref[...])
    folded = jnp.dot(rows, low, preferred_element_type=jnp.float32)
    folded = folded + jnp.dot(rows, high, preferred_element_type=jnp.float32)
    peak = jnp.max(jnp.abs(folded), axis=1, keepdims=True)
    exponent = jnp.zeros_like(peak)
    for bit in SHIFTS:
        fits = (peak * (2.0 ** bit) < TOP) & (exponent + bit <= 96)
        peak = jnp.where(fits, peak * (2.0 ** bit), peak)
        exponent = jnp.where(fits, exponent + bit, exponent)
    scaled = folded * power(exponent, 1) * (2.0 ** FRACTION)
    codes = jnp.clip(jnp.round(scaled), -32767.0, 32767.0)
    count = rows.shape[0]
    out_ref[:count] = codes.astype(jnp.int32).astype(jnp.int16)
    across = jnp.transpose(jnp.broadcast_to(exponent, (count, LANES)))
    out_ref[count:] = across[:PAD].astype(jnp.int32).astype(jnp.int16)


def fold(slabs, transform):
    rows, cols = slabs.shape[0], transform.shape[1]
    return pl.pallas_call(
        fold_kernel,
        out_shape=jax.ShapeDtypeStruct((rows + PAD, cols), jnp.int16),
        compiler_params=pltpu.CompilerParams(vmem_limit_bytes=VMEM),
        cost_estimate=pl.CostEstimate(flops=4 * rows * slabs.shape[1] * cols, bytes_accessed=4 << 20, transcendentals=0),
        name="fold",
    )(slabs, transform)


def pick_kernel(per_device, width, sizes_ref, rep_ref, tau_hbm, out_hbm, low_ref, turn_ref, left_ref, tau_ref, stage_ref, tau_sem, out_sem):
    slabs, packed, groups = sizes_ref.shape[0], tau_ref.shape[1], stage_ref.shape[0]
    load = pltpu.make_async_copy(tau_hbm, tau_ref, tau_sem)
    load.start()
    start = rep_ref[0] * width

    def place(s, base):
        low = jnp.minimum((base + start) & -LANES, packed - 2 * LANES)
        low_ref[s] = low
        turn_ref[s] = 2 * LANES - jnp.minimum(base + start - low, 2 * LANES - 1)
        size = sizes_ref[s]
        left_ref[s] = size - start
        return base + size

    lax.fori_loop(0, slabs, place, jnp.int32(0), unroll=16)
    load.wait()
    lane = lax.broadcasted_iota(jnp.int32, (tau_ref.shape[0], LANES), 1)
    stores = []
    for group in range(groups):
        for n in range(slabs // groups):
            slab = (n // per_device * groups + group) * per_device + n % per_device
            window = tau_ref[:, pl.ds(pl.multiple_of(low_ref[slab], LANES), 2 * LANES)]
            moved = pltpu.roll(window, turn_ref[slab], axis=1)[:, :LANES]
            stage_ref[group, :, n * LANES:(n + 1) * LANES] = jnp.where(lane < left_ref[slab], moved, jnp.zeros_like(moved))
        store = pltpu.make_async_copy(stage_ref.at[group], out_hbm.at[group], out_sem.at[group])
        store.start()
        stores.append(store)
    for store in stores:
        store.wait()


def pick(tau, sizes, rep, groups, per_device, width):
    slabs = sizes.shape[0]
    shape = (groups, tau.shape[0], slabs // groups * width)
    return pl.pallas_call(
        functools.partial(pick_kernel, per_device, width),
        in_specs=[pl.BlockSpec(memory_space=pltpu.SMEM)] * 2 + [pl.BlockSpec(memory_space=pl.ANY)],
        out_specs=pl.BlockSpec(memory_space=pl.ANY),
        out_shape=jax.ShapeDtypeStruct(shape, jnp.bfloat16),
        scratch_shapes=[pltpu.SMEM((slabs,), jnp.int32)] * 3
        + [
            pltpu.VMEM(tau.shape, jnp.bfloat16),
            pltpu.VMEM(shape, jnp.bfloat16),
            pltpu.SemaphoreType.DMA,
            pltpu.SemaphoreType.DMA((groups,)),
        ],
        compiler_params=pltpu.CompilerParams(vmem_limit_bytes=VMEM),
        cost_estimate=pl.CostEstimate(flops=0, bytes_accessed=12 << 20, transcendentals=0),
        name="pick",
    )(sizes, rep, tau)


def contract_kernel(amps_ref, coded_ref, out_ref):
    chunks, depth = coded_ref.shape[0], coded_ref.shape[1] - PAD

    @pl.when(pl.program_id(0) == 0)
    def _():
        out_ref[...] = jnp.zeros_like(out_ref)

    part = None
    for n in range(chunks):
        code = coded_ref[n, :depth].astype(jnp.int32).astype(jnp.float32)
        exponent = coded_ref[n, depth:].astype(jnp.int32).astype(jnp.float32)[:1]
        scale = power(exponent, -1) * (2.0 ** -FRACTION)
        amps = (amps_ref[:, n * depth:(n + 1) * depth].astype(jnp.float32) * scale).astype(jnp.bfloat16)
        for term in split2(code):
            more = jnp.dot(amps, term, preferred_element_type=jnp.float32)
            part = more if part is None else part + more
    groups, reps, rows, cols = out_ref.shape
    for g in range(groups):
        for r in range(reps):
            out_ref[g, r] += part[g * rows:(g + 1) * rows, r * cols:(r + 1) * cols]


def contract(amps, coded, groups, reps):
    chunks, padded, cols = coded.shape
    depth = padded - PAD
    step = 2
    shape = (groups, reps, amps.shape[0] // groups, cols // reps)
    return pl.pallas_call(
        contract_kernel,
        grid=(chunks // step,),
        in_specs=[
            pl.BlockSpec((amps.shape[0], step * depth), lambda k: (0, k)),
            pl.BlockSpec((step, padded, cols), lambda k: (k, 0, 0)),
        ],
        out_specs=pl.BlockSpec(shape, lambda k: (0, 0, 0, 0)),
        out_shape=jax.ShapeDtypeStruct(shape, jnp.float32),
        compiler_params=pltpu.CompilerParams(vmem_limit_bytes=VMEM),
        cost_estimate=pl.CostEstimate(flops=4 * amps.size * cols, bytes_accessed=9 << 20, transcendentals=0),
        name="contract",
    )(amps, coded)


def body(tau_ao, slab_sizes, integrals, transform):
    groups = lax.axis_size("y") * lax.axis_size("core")
    reps = lax.axis_size("rep")
    per_device, width, depth = integrals.shape
    coded = fold(integrals.reshape(per_device * width, depth), transform)
    line = lax.all_gather(coded, "z", axis=0, tiled=False)
    rep = lax.axis_index("rep").reshape(1)
    picked = pick(tau_ao, slab_sizes, rep, groups, per_device, width)
    arrived = lax.all_to_all(picked, ("y", "core"), split_axis=0, concat_axis=0, tiled=True)
    amps = arrived.reshape(-1, arrived.shape[-1])
    partial = contract(amps, line, groups, reps)
    partial = partial.reshape(groups * reps, *partial.shape[2:])
    shares = lax.all_to_all(partial, ("y", "core", "rep"), split_axis=0, concat_axis=0, tiled=True)
    return jnp.sum(shares, axis=0)


def solution(mesh):
    fine = Mesh(mesh.devices.reshape(8, 4, 2, 4), ("z", "y", "core", "rep"))
    pair = ("z", "y", "core")
    return jax.shard_map(
        body,
        mesh=fine,
        in_specs=(P(pair, None), P(), P(pair, "rep", None), P()),
        out_specs=P(pair, "rep"),
        check_vma=False,
    )
```

time: 126 us -> 99.9 us (0.79)
  Pallas kernels: 46.8 us -> 20.3 us
    pallas_call x2, Pallas kernels: 41.3 us -> 15.5 us  [the longest x1 8.28 us: contract(): pl.pallas_call(contract_kernel, grid=(chunks // step,), in_specs=[pl.Bloc...]
  transfers between devices with their start and end apart: 1 -> 1, of which waited for: 0 -> 0; matrix products, arithmetic and copies ran while one was open for 0% -> 0% of each run, Pallas kernels for 4% -> 5%
where the time goes in v2:
time: 99.9 us; the launch traced here: 99.5 us
  blocking collectives  70.8 us (71%)
  Pallas kernels  20.3 us (20%)
  starting transfers between devices  7.68 us (8%)
    all_gather x1, blocking collectives, body(): line = lax.all_gather(coded, 'z', axis=0, tiled=False)  46.9 us
    all_to_all x1, blocking collectives, body(): lax.all_to_all(partial, ('y', 'core', 'rep'), split_axis=0, concat_axis=0...  23.9 us
    pallas_call x1, Pallas kernels, contract(): pl.pallas_call(contract_kernel, grid=(chunks // step,), in_specs=[pl.Bloc...  8.28 us
    all_to_all x1, starting transfers between devices, body(): lax.all_to_all(picked, ('y', 'core'), split_axis=0, concat_axis=0, tiled=...  7.68 us
    pallas_call x1, Pallas kernels, pick(): pl.pallas_call(functools.partial(pick_kernel, per_device, width), in_spec...  7.18 us
    pallas_call x1, Pallas kernels, fold(): pl.pallas_call(fold_kernel, out_shape=jax.ShapeDtypeStruct((rows + PAD, c...  4.83 us
  transfers between devices with their start and end apart: 1, of which 0 were waited for; matrix products, arithmetic and copies ran while one was open for 0% of the time, Pallas kernels for 5%

profile of v2, /device:TPU:1, one launch (start us, length us, event | category | flops | bytes accessed | tf_op | source)
XLA Modules:
  0.0 99.5 jit_solution(5231884149877068473)
XLA Ops:
  0.0 7.2 %pick.1 = bf16[8,64,4096]{2,1,0:T(8,128)(2,1)} custom-call(s32[256]{0:T(256)} %sizes_ref.1, s32[1]{0:T(128)} %bitcast.rep_ref, bf16[64,65536]{1,0:T(8,128)(2,1)} %tau_hbm.1), custom_call_target="tpu_custom_call" | custom-call | bytes 12582912 | tf_op jit(solution)/shard_map/pick/pallas_call | solution.py:97
  7.2 7.7 %all-to-all-start = ((bf16[8,64,4096]{2,1,0:T(8,128)(2,1)}), bf16[8,64,4096]{2,1,0:T(8,128)(2,1)}, u32[]{:S(2)}, u32[]{:S(2)}) async-start(bf16[8,64,4096]{2,1,0:T(8,128)(2,1)} %pick.1), calls=%async_computation | async-start | bytes 8388608 | tf_op jit(solution)/shard_map/all_to_all | solution.py:165
  14.9 4.8 %fold.1 = s16[528,512]{1,0:T(8,128)(2,1)} custom-call(bf16[512,1024]{1,0:T(8,128)(2,1)} %bitcast.7, f32[1024,512]{1,0:T(8,128)} %transform_ref.1), custom_call_target="tpu_custom_call" | custom-call | flops 1073741824 | bytes 4194304 | tf_op jit(solution)/shard_map/fold/pallas_call | solution.py:54
  19.7 46.9 %all-gather.2 = s16[4224,512]{1,0:T(8,128)(2,1)} all-gather(s16[528,512]{1,0:T(8,128)(2,1)} %fold.1), channel_id=2, replica_groups=mesh['z'=8,'y'=4,'core'=2,'rep'=4] {'z'}, dimensions={0}, use_global_device_ids=true | all-gather | bytes 4866048 | tf_op jit(solution)/shard_map/all_gather | solution.py:162
  66.6 0.0 all-to-all-done
  66.6 8.3 %contract.1 = f32[8,4,64,128]{3,2,1,0:T(8,128)} custom-call(bf16[512,4096]{1,0:T(8,128)(2,1)} %bitcast.1.amps_ref, s16[8,528,512]{2,1,0:T(8,128)(2,1)} %bitcast.5), custom_call_target="tpu_custom_call" | custom-call | flops 4294967296 | bytes 9437184 | tf_op jit(solution)/shard_map/contract/pallas_call | solution.py:142
  74.9 23.9 %all_to_all.10 = f32[32,64,128]{2,1,0:T(8,128)S(1)} all-to-all(f32[32,64,128]{2,1,0:T(8,128)} %bitcast.6), channel_id=1, replica_groups=mesh['z'=8,'y'=4,'core'=2,'rep'=4] {'y','core','rep'}, dimensions={0} | all-to-all | bytes 2097152 | tf_op jit(solution)/shard_map/all_to_all | solution.py:169
  98.8 0.7 reduce_sum.9
Async XLA Ops:
  7.2 59.4 %all-to-all-start = ((bf16[8,64,4096]{2,1,0:T(8,128)(2,1)}), bf16[8,64,4096]{2,1,0:T(8,128)(2,1)}, u32[]{:S(2)}, u32[]{:S(2)}) async-start(bf16[8,64,4096]{2,1,0:T(8,128)(2,1)} %pick.1), calls=%async_computation | async-start | bytes 8388608 | tf_op jit(solution)/shard_map/all_to_all | solution.py:165

commit v3 on v2

v3 whole, which is shorter than its diff:
```python
import functools

import jax
import jax.numpy as jnp
from jax import lax
from jax.experimental import pallas as pl
from jax.experimental.pallas import tpu as pltpu
from jax.sharding import Mesh
from jax.sharding import PartitionSpec as P

LANES = 128
PAD = 16
VMEM = 56 * 1024 * 1024
SHIFTS = (64, 32, 16, 8, 4, 2, 1)
TOP = 8.0
FRACTION = 12


def power(exponent, sign):
    out = jnp.ones_like(exponent)
    for bit in SHIFTS:
        has = exponent >= bit
        out = jnp.where(has, out * (2.0 ** (sign * bit)), out)
        exponent = jnp.where(has, exponent - bit, exponent)
    return out


def split2(value):
    first = value.astype(jnp.bfloat16)
    return first, (value - first.astype(jnp.float32)).astype(jnp.bfloat16)


def fold_kernel(slab_ref, transform_ref, out_ref):
    rows = slab_ref[...]
    high, low = split2(transform_ref[...])
    folded = jnp.dot(rows, low, preferred_element_type=jnp.float32)
    folded = folded + jnp.dot(rows, high, preferred_element_type=jnp.float32)
    peak = jnp.max(jnp.abs(folded), axis=1, keepdims=True)
    exponent = jnp.zeros_like(peak)
    for bit in SHIFTS:
        fits = (peak * (2.0 ** bit) < TOP) & (exponent + bit <= 96)
        peak = jnp.where(fits, peak * (2.0 ** bit), peak)
        exponent = jnp.where(fits, exponent + bit, exponent)
    scaled = folded * power(exponent, 1) * (2.0 ** FRACTION)
    codes = jnp.clip(jnp.round(scaled), -32767.0, 32767.0)
    count = rows.shape[0]
    out_ref[:count] = codes.astype(jnp.int32).astype(jnp.int16)
    across = jnp.transpose(jnp.broadcast_to(exponent, (count, LANES)))
    out_ref[count:] = across[:PAD].astype(jnp.int32).astype(jnp.int16)


def fold(slabs, transform):
    rows, cols = slabs.shape[0], transform.shape[1]
    return pl.pallas_call(
        fold_kernel,
        out_shape=jax.ShapeDtypeStruct((rows + PAD, cols), jnp.int16),
        compiler_params=pltpu.CompilerParams(vmem_limit_bytes=16 << 20),
        cost_estimate=pl.CostEstimate(flops=4 * rows * slabs.shape[1] * cols, bytes_accessed=4 << 20, transcendentals=0),
        name="fold",
    )(slabs, transform)


def pick_kernel(per_device, width, sizes_ref, rep_ref, tau_hbm, out_hbm, low_ref, turn_ref, left_ref, tau_ref, stage_ref, tau_sems, out_sems):
    slabs, packed, groups = sizes_ref.shape[0], tau_ref.shape[1], stage_ref.shape[0]
    pieces, lines = tau_sems.shape[0], out_sems.shape[0]
    piece, span = packed // pieces, per_device * width

    def load(k):
        columns = pl.ds(pl.multiple_of(k * piece, piece), piece)
        return pltpu.make_async_copy(tau_hbm.at[:, columns], tau_ref.at[:, columns], tau_sems.at[k])

    for k in range(pieces):
        load(k).start()
    start = rep_ref[0] * width

    def place(s, base):
        low = jnp.minimum((base + start) & -LANES, packed - 2 * LANES)
        low_ref[s] = low
        turn_ref[s] = 2 * LANES - jnp.minimum(base + start - low, 2 * LANES - 1)
        size = sizes_ref[s]
        left_ref[s] = size - start
        return base + size

    lax.fori_loop(0, slabs, place, jnp.int32(0), unroll=16)
    lane = lax.broadcasted_iota(jnp.int32, (tau_ref.shape[0], LANES), 1)

    def arrive(k, carry):
        load(k).wait()
        return carry

    stores, have = [], jnp.int32(0)
    for z in range(lines):
        end = low_ref[(z + 1) * groups * per_device - 1] + 2 * LANES
        need = lax.div(end + piece - 1, piece) if z < lines - 1 else jnp.int32(pieces)
        lax.fori_loop(have, need, arrive, 0)
        have = need
        for group in range(groups):
            for i in range(per_device):
                slab = (z * groups + group) * per_device + i
                column = z * span + i * width
                window = tau_ref[:, pl.ds(pl.multiple_of(low_ref[slab], LANES), 2 * LANES)]
                moved = pltpu.roll(window, turn_ref[slab], axis=1)[:, :LANES]
                stage_ref[group, :, column:column + LANES] = jnp.where(lane < left_ref[slab], moved, jnp.zeros_like(moved))
        columns = pl.ds(z * span, span)
        store = pltpu.make_async_copy(stage_ref.at[:, :, columns], out_hbm.at[:, :, columns], out_sems.at[z])
        store.start()
        stores.append(store)
    for store in stores:
        store.wait()


def pick(tau, sizes, rep, groups, per_device, width):
    slabs = sizes.shape[0]
    lines = slabs // groups // per_device
    shape = (groups, tau.shape[0], lines * per_device * width)
    return pl.pallas_call(
        functools.partial(pick_kernel, per_device, width),
        in_specs=[pl.BlockSpec(memory_space=pltpu.SMEM)] * 2 + [pl.BlockSpec(memory_space=pl.ANY)],
        out_specs=pl.BlockSpec(memory_space=pl.ANY),
        out_shape=jax.ShapeDtypeStruct(shape, jnp.bfloat16),
        scratch_shapes=[pltpu.SMEM((slabs,), jnp.int32)] * 3
        + [
            pltpu.VMEM(tau.shape, jnp.bfloat16),
            pltpu.VMEM(shape, jnp.bfloat16),
            pltpu.SemaphoreType.DMA((8,)),
            pltpu.SemaphoreType.DMA((lines,)),
        ],
        compiler_params=pltpu.CompilerParams(vmem_limit_bytes=VMEM),
        cost_estimate=pl.CostEstimate(flops=0, bytes_accessed=12 << 20, transcendentals=0),
        name="pick",
    )(sizes, rep, tau)


def contract_kernel(step, core_ref, amps_hbm, coded_hbm, out_ref, amps_ref, coded_ref, amps_sems, coded_sems):
    chunks, depth = coded_ref.shape[0], coded_ref.shape[1] - PAD
    ys, reps, rows, cols = out_ref.shape
    stride = amps_hbm.shape[0] // ys
    loads = []
    for n in range(chunks // step):
        columns = pl.ds(n * step * depth, step * depth)
        load = [pltpu.make_async_copy(coded_hbm.at[pl.ds(n * step, step)], coded_ref.at[pl.ds(n * step, step)], coded_sems.at[n])]
        for y in range(ys):
            source = amps_hbm.at[y * stride + core_ref[0], :, columns]
            load.append(pltpu.make_async_copy(source, amps_ref.at[y, :, columns], amps_sems.at[n, y]))
        loads.append(load)
    for load in loads:
        for copy in load:
            copy.start()
    total = None
    for n, load in enumerate(loads):
        for copy in load:
            copy.wait()
        for k in range(n * step, (n + 1) * step):
            code = coded_ref[k, :depth].astype(jnp.int32).astype(jnp.float32)
            exponent = coded_ref[k, depth:].astype(jnp.int32).astype(jnp.float32)[:1]
            scale = power(exponent, -1) * (2.0 ** -FRACTION)
            amps = amps_ref[:, :, k * depth:(k + 1) * depth].reshape(ys * rows, depth)
            amps = (amps.astype(jnp.float32) * scale).astype(jnp.bfloat16)
            for term in split2(code):
                more = jnp.dot(amps, term, preferred_element_type=jnp.float32)
                total = more if total is None else total + more
    for y in range(ys):
        for r in range(reps):
            out_ref[y, r] = total[y * rows:(y + 1) * rows, r * cols:(r + 1) * cols]


def contract(amps, coded, core, ys, reps, grant):
    chunks, padded, cols = coded.shape
    groups, rows, depth = amps.shape
    step = 2
    shape = (ys, reps, rows, cols // reps)
    return pl.pallas_call(
        functools.partial(contract_kernel, step),
        in_specs=[pl.BlockSpec(memory_space=pltpu.SMEM)] + [pl.BlockSpec(memory_space=pl.ANY)] * 2,
        out_specs=pl.BlockSpec(memory_space=pltpu.VMEM),
        out_shape=jax.ShapeDtypeStruct(shape, jnp.float32),
        scratch_shapes=[
            pltpu.VMEM((ys, rows, depth), jnp.bfloat16),
            pltpu.VMEM(coded.shape, jnp.int16),
            pltpu.SemaphoreType.DMA((chunks // step, ys)),
            pltpu.SemaphoreType.DMA((chunks // step,)),
        ],
        compiler_params=pltpu.CompilerParams(vmem_limit_bytes=grant << 20),
        cost_estimate=pl.CostEstimate(flops=4 * ys * rows * depth * cols, bytes_accessed=7 << 20, transcendentals=0),
        name="contract",
    )(core.reshape(1), amps, coded)


def body(tau_ao, slab_sizes, integrals, transform):
    groups = lax.axis_size("y") * lax.axis_size("core")
    reps = lax.axis_size("rep")
    per_device, width, depth = integrals.shape
    coded = fold(integrals.reshape(per_device * width, depth), transform)
    line = lax.all_gather(coded, "z", axis=0, tiled=False)
    rep = lax.axis_index("rep").reshape(1)
    picked = pick(tau_ao, slab_sizes, rep, groups, per_device, width)
    arrived = lax.all_to_all(picked, ("y", "core"), split_axis=0, concat_axis=0, tiled=True)
    core, ys = lax.axis_index("core"), lax.axis_size("y")
    theirs = contract(arrived, line, 1 - core, ys, reps, 50)
    theirs = lax.ppermute(theirs, "core", [(0, 1), (1, 0)])
    partial = contract(arrived, line, core, ys, reps, 32) + theirs
    partial = partial.reshape(ys * reps, *partial.shape[2:])
    shares = lax.all_to_all(partial, ("y", "rep"), split_axis=0, concat_axis=0, tiled=True)
    return jnp.sum(shares, axis=0)


def solution(mesh):
    fine = Mesh(mesh.devices.reshape(8, 4, 2, 4), ("z", "y", "core", "rep"))
    pair = ("z", "y", "core")
    return jax.shard_map(
        body,
        mesh=fine,
        in_specs=(P(pair, None), P(), P(pair, "rep", None), P()),
        out_specs=P(pair, "rep"),
        check_vma=False,
    )
```

time: 99.9 us -> 92.3 us (0.924)
  blocking collectives: 70.8 us -> 64 us
  Pallas kernels: 20.3 us -> 18.2 us
  starting transfers between devices: 7.68 us -> 8.9 us
    all_to_all x1, blocking collectives: 23.9 us -> 17.3 us  [body(): lax.all_to_all(partial, ('y', 'rep'), split_axis=0, concat_axis=0, tiled=...]
    pallas_call x1, Pallas kernels: 4.83 us -> 2.08 us  [fold(): pl.pallas_call(fold_kernel, out_shape=jax.ShapeDtypeStruct((rows + PAD, c...]
    pallas_call x1 -> x2, Pallas kernels: 8.28 us -> 9.48 us  [contract(): pl.pallas_call(functools.partial(contract_kernel, step), in_specs=[pl.Blo...]
  transfers between devices with their start and end apart: 1 -> 2, of which waited for: 0 -> 1; matrix products, arithmetic and copies ran while one was open for 0% -> 0% of each run, Pallas kernels for 5% -> 7%
where the time goes in v3:
time: 92.3 us; the launch traced here: 92 us
  blocking collectives  64 us (69%)
  Pallas kernels  18.2 us (20%)
  starting transfers between devices  8.9 us (10%)
    all_gather x1, blocking collectives, body(): line = lax.all_gather(coded, 'z', axis=0, tiled=False)  46.7 us
    all_to_all x1, blocking collectives, body(): lax.all_to_all(partial, ('y', 'rep'), split_axis=0, concat_axis=0, tiled=...  17.3 us
    pallas_call x2, Pallas kernels, contract(): pl.pallas_call(functools.partial(contract_kernel, step), in_specs=[pl.Blo...  9.48 us
    all_to_all x1, starting transfers between devices, body(): lax.all_to_all(picked, ('y', 'core'), split_axis=0, concat_axis=0, tiled=...  7.94 us
    pallas_call x1, Pallas kernels, pick(): pl.pallas_call(functools.partial(pick_kernel, per_device, width), in_spec...  6.67 us
    pallas_call x1, Pallas kernels, fold(): pl.pallas_call(fold_kernel, out_shape=jax.ShapeDtypeStruct((rows + PAD, c...  2.08 us
  transfers between devices with their start and end apart: 2, of which 1 were waited for; matrix products, arithmetic and copies ran while one was open for 0% of the time, Pallas kernels for 7%

profile of v3, /device:TPU:1, one launch (start us, length us, event | category | flops | bytes accessed | tf_op | source)
XLA Modules:
  0.0 92.0 jit_solution(14081094549679075996)
XLA Ops:
  0.0 6.7 %pick.1 = bf16[8,64,4096]{2,1,0:T(8,128)(2,1)} custom-call(s32[256]{0:T(256)} %sizes_ref.1, s32[1]{0:T(128)} %bitcast.1.rep_ref, bf16[64,65536]{1,0:T(8,128)(2,1)} %tau_hbm.1), custom_call_target="tpu_custom_call" | custom-call | bytes 12582912 | tf_op jit(solution)/shard_map/pick/pallas_call | solution.py:116
  6.7 0.0 copy-start.1
  6.7 0.0 copy-start.2
  6.7 7.9 %all-to-all-start = ((bf16[8,64,4096]{2,1,0:T(8,128)(2,1)}), bf16[8,64,4096]{2,1,0:T(8,128)(2,1)}, u32[]{:S(2)}, u32[]{:S(2)}) async-start(bf16[8,64,4096]{2,1,0:T(8,128)(2,1)} %pick.1), calls=%async_computation | async-start | bytes 8388608 | tf_op jit(solution)/shard_map/all_to_all | solution.py:197
  14.6 0.0 copy-done.1
  14.7 0.0 copy-done.2
  14.7 2.1 %fold.1 = s16[528,512]{1,0:T(8,128)(2,1)S(1)} custom-call(bf16[512,1024]{1,0:T(8,128)(2,1)S(1)} %bitcast.8, f32[1024,512]{1,0:T(8,128)S(1)} %copy-done.1), custom_call_target="tpu_custom_call" | custom-call | flops 1073741824 | bytes 4194304 | tf_op jit(solution)/shard_map/fold/pallas_call | solution.py:54
  16.7 46.7 %all-gather.2 = s16[4224,512]{1,0:T(8,128)(2,1)} all-gather(s16[528,512]{1,0:T(8,128)(2,1)S(1)} %fold.1), channel_id=2, replica_groups=mesh['z'=8,'y'=4,'core'=2,'rep'=4] {'z'}, dimensions={0}, use_global_device_ids=true | all-gather | bytes 4866048 | tf_op jit(solution)/shard_map/all_gather | solution.py:194
  63.4 0.1 all-to-all-done.amps_hbm
  63.6 0.0 copy-start
  63.6 5.1 %contract.3 = f32[4,4,64,128]{3,2,1,0:T(8,128)S(1)} custom-call(s32[1]{0:T(128)} %bitcast.4.core_ref, bf16[8,64,4096]{2,1,0:T(8,128)(2,1)} %all-to-all-done.amps_hbm, s16[8,528,512]{2,1,0:T(8,128)(2,1)} %bitcast.6), custom_call_target="tpu_custom_call" | custom-call | flops 2147483648 | bytes 7340032 | tf_op jit(solution)/shard_map/contract/pallas_call | solution.py:172
  68.7 1.0 %collective-permute-start = (f32[4,4,64,128]{3,2,1,0:T(8,128)S(1)}, f32[4,4,64,128]{3,2,1,0:T(8,128)S(1)}, u32[]{:S(2)}, u32[]{:S(2)}) collective-permute-start(f32[4,4,64,128]{3,2,1,0:T(8,128)S(1)} %contract.3), channel_id=1, source_target_pairs={{0,4},{4,0},{1,5},{5,1},{2,6},{6,2},{3,7},{7,3},{8,12},{12,8},{9,1... | collective-permute-start | bytes 1572872 | tf_op jit(solution)/shard_map/ppermute | solution.py:200
  69.7 0.0 copy-done
  69.7 4.4 %contract.2 = f32[4,4,64,128]{3,2,1,0:T(8,128)S(1)} custom-call(s32[1]{0:T(128)} %bitcast.core_ref, bf16[8,64,4096]{2,1,0:T(8,128)(2,1)} %all-to-all-done.amps_hbm, s16[8,528,512]{2,1,0:T(8,128)(2,1)S(1)} %bitcast.7), custom_call_target="tpu_custom_call" | custom-call | flops 2147483648 | bytes 7340032 | tf_op jit(solution)/shard_map/contract/pallas_call | solution.py:172
  74.0 0.0 collective-permute-done
  74.0 0.1 add.3
  74.1 17.3 %all_to_all.10 = f32[16,64,128]{2,1,0:T(8,128)S(1)} all-to-all(f32[16,64,128]{2,1,0:T(8,128)S(1)} %bitcast.9), channel_id=1, replica_groups=mesh['z'=8,'y'=4,'core'=2,'rep'=4] {'y','rep'}, dimensions={0} | all-to-all | bytes 1048576 | tf_op jit(solution)/shard_map/all_to_all | solution.py:203
  91.4 0.6 reduce_sum.9
Async XLA Ops:
  6.7 8.0 %copy-start.1 = (f32[1024,512]{1,0:T(8,128)S(1)}, f32[1024,512]{1,0:T(8,128)}, u32[]{:S(2)}) copy-start(f32[1024,512]{1,0:T(8,128)} %transform_ref.1) | copy-start | bytes 6291460
  6.7 8.0 %copy-start.2 = (bf16[4,128,1024]{2,1,0:T(8,128)(2,1)S(1)}, bf16[4,128,1024]{2,1,0:T(8,128)(2,1)}, u32[]{:S(2)}) copy-start(bf16[4,128,1024]{2,1,0:T(8,128)(2,1)} %param.6) | copy-start | bytes 3145732
  6.7 56.9 %all-to-all-start = ((bf16[8,64,4096]{2,1,0:T(8,128)(2,1)}), bf16[8,64,4096]{2,1,0:T(8,128)(2,1)}, u32[]{:S(2)}, u32[]{:S(2)}) async-start(bf16[8,64,4096]{2,1,0:T(8,128)(2,1)} %pick.1), calls=%async_computation | async-start | bytes 8388608 | tf_op jit(solution)/shard_map/all_to_all | solution.py:197
  63.6 6.1 %copy-start = (s16[4224,512]{1,0:T(8,128)(2,1)S(1)}, s16[4224,512]{1,0:T(8,128)(2,1)}, u32[]{:S(2)}) copy-start(s16[4224,512]{1,0:T(8,128)(2,1)} %all-gather.2) | copy-start | bytes 12976132
  68.7 5.3 %collective-permute-start = (f32[4,4,64,128]{3,2,1,0:T(8,128)S(1)}, f32[4,4,64,128]{3,2,1,0:T(8,128)S(1)}, u32[]{:S(2)}, u32[]{:S(2)}) collective-permute-start(f32[4,4,64,128]{3,2,1,0:T(8,128)S(1)} %contract.3), channel_id=1, source_target_pairs={{0,4},{4,0},{1,5},{5,1},{2,6},{6,2},{3,7},{7,3},{8,12},{12,8},{9,1... | collective-permute-start | bytes 1572872 | tf_op jit(solution)/shard_map/ppermute | solution.py:200

commit v4 on v3

--- a/solution.py
+++ b/solution.py
@@ -155,7 +155,7 @@
             exponent = coded_ref[k, depth:].astype(jnp.int32).astype(jnp.float32)[:1]
             scale = power(exponent, -1) * (2.0 ** -FRACTION)
             amps = amps_ref[:, :, k * depth:(k + 1) * depth].reshape(ys * rows, depth)
-            amps = (amps.astype(jnp.float32) * scale).astype(jnp.bfloat16)
+            amps = amps * scale.astype(jnp.bfloat16)
             for term in split2(code):
                 more = jnp.dot(amps, term, preferred_element_type=jnp.float32)
                 total = more if total is None else total + more

time: 92.3 us -> 91.9 us (level)
  no operation moved by 1% of the time
where the time goes in v4:
time: 91.9 us; the launch traced here: 91.5 us
  blocking collectives  64.1 us (70%)
  Pallas kernels  17.6 us (19%)
  starting transfers between devices  8.91 us (10%)
    all_gather x1, blocking collectives, body(): line = lax.all_gather(coded, 'z', axis=0, tiled=False)  46.7 us
    all_to_all x1, blocking collectives, body(): lax.all_to_all(partial, ('y', 'rep'), split_axis=0, concat_axis=0, tiled=...  17.4 us
    pallas_call x2, Pallas kernels, contract(): pl.pallas_call(functools.partial(contract_kernel, step), in_specs=[pl.Blo...  9.34 us
    all_to_all x1, starting transfers between devices, body(): lax.all_to_all(picked, ('y', 'core'), split_axis=0, concat_axis=0, tiled=...  7.94 us
    pallas_call x1, Pallas kernels, pick(): pl.pallas_call(functools.partial(pick_kernel, per_device, width), in_spec...  6.14 us
    pallas_call x1, Pallas kernels, fold(): pl.pallas_call(fold_kernel, out_shape=jax.ShapeDtypeStruct((rows + PAD, c...  2.08 us
  transfers between devices with their start and end apart: 2, of which 1 were waited for; matrix products, arithmetic and copies ran while one was open for 0% of the time, Pallas kernels for 7%

profile of v4, /device:TPU:1, one launch (start us, length us, event | category | flops | bytes accessed | tf_op | source)
XLA Modules:
  0.0 91.5 jit_solution(10930790326809022827)
XLA Ops:
  0.0 6.1 %pick.1 = bf16[8,64,4096]{2,1,0:T(8,128)(2,1)} custom-call(s32[256]{0:T(256)} %sizes_ref.1, s32[1]{0:T(128)} %bitcast.1.rep_ref, bf16[64,65536]{1,0:T(8,128)(2,1)} %tau_hbm.1), custom_call_target="tpu_custom_call" | custom-call | bytes 12582912 | tf_op jit(solution)/shard_map/pick/pallas_call | solution.py:116
  6.2 0.0 copy-start.1
  6.2 0.0 copy-start.2
  6.2 7.9 %all-to-all-start = ((bf16[8,64,4096]{2,1,0:T(8,128)(2,1)}), bf16[8,64,4096]{2,1,0:T(8,128)(2,1)}, u32[]{:S(2)}, u32[]{:S(2)}) async-start(bf16[8,64,4096]{2,1,0:T(8,128)(2,1)} %pick.1), calls=%async_computation | async-start | bytes 8388608 | tf_op jit(solution)/shard_map/all_to_all | solution.py:197
  14.1 0.0 copy-done.1
  14.1 0.0 copy-done.2
  14.1 2.1 %fold.1 = s16[528,512]{1,0:T(8,128)(2,1)S(1)} custom-call(bf16[512,1024]{1,0:T(8,128)(2,1)S(1)} %bitcast.8, f32[1024,512]{1,0:T(8,128)S(1)} %copy-done.1), custom_call_target="tpu_custom_call" | custom-call | flops 1073741824 | bytes 4194304 | tf_op jit(solution)/shard_map/fold/pallas_call | solution.py:54
  16.2 46.7 %all-gather.2 = s16[4224,512]{1,0:T(8,128)(2,1)} all-gather(s16[528,512]{1,0:T(8,128)(2,1)S(1)} %fold.1), channel_id=2, replica_groups=mesh['z'=8,'y'=4,'core'=2,'rep'=4] {'z'}, dimensions={0}, use_global_device_ids=true | all-gather | bytes 4866048 | tf_op jit(solution)/shard_map/all_gather | solution.py:194
  62.9 0.1 all-to-all-done.amps_hbm
  63.0 0.0 copy-start
  63.1 5.0 %contract.3 = f32[4,4,64,128]{3,2,1,0:T(8,128)S(1)} custom-call(s32[1]{0:T(128)} %bitcast.4.core_ref, bf16[8,64,4096]{2,1,0:T(8,128)(2,1)} %all-to-all-done.amps_hbm, s16[8,528,512]{2,1,0:T(8,128)(2,1)} %bitcast.6), custom_call_target="tpu_custom_call" | custom-call | flops 2147483648 | bytes 7340032 | tf_op jit(solution)/shard_map/contract/pallas_call | solution.py:172
  68.1 1.0 %collective-permute-start = (f32[4,4,64,128]{3,2,1,0:T(8,128)S(1)}, f32[4,4,64,128]{3,2,1,0:T(8,128)S(1)}, u32[]{:S(2)}, u32[]{:S(2)}) collective-permute-start(f32[4,4,64,128]{3,2,1,0:T(8,128)S(1)} %contract.3), channel_id=1, source_target_pairs={{0,4},{4,0},{1,5},{5,1},{2,6},{6,2},{3,7},{7,3},{8,12},{12,8},{9,1... | collective-permute-start | bytes 1572872 | tf_op jit(solution)/shard_map/ppermute | solution.py:200
  69.1 0.0 copy-done
  69.1 4.3 %contract.2 = f32[4,4,64,128]{3,2,1,0:T(8,128)S(1)} custom-call(s32[1]{0:T(128)} %bitcast.core_ref, bf16[8,64,4096]{2,1,0:T(8,128)(2,1)} %all-to-all-done.amps_hbm, s16[8,528,512]{2,1,0:T(8,128)(2,1)S(1)} %bitcast.7), custom_call_target="tpu_custom_call" | custom-call | flops 2147483648 | bytes 7340032 | tf_op jit(solution)/shard_map/contract/pallas_call | solution.py:172
  73.4 0.0 collective-permute-done
  73.4 0.1 add.3
  73.5 17.4 %all_to_all.10 = f32[16,64,128]{2,1,0:T(8,128)S(1)} all-to-all(f32[16,64,128]{2,1,0:T(8,128)S(1)} %bitcast.9), channel_id=1, replica_groups=mesh['z'=8,'y'=4,'core'=2,'rep'=4] {'y','rep'}, dimensions={0} | all-to-all | bytes 1048576 | tf_op jit(solution)/shard_map/all_to_all | solution.py:203
  90.9 0.6 reduce_sum.9
Async XLA Ops:
  6.2 8.0 %copy-start.1 = (f32[1024,512]{1,0:T(8,128)S(1)}, f32[1024,512]{1,0:T(8,128)}, u32[]{:S(2)}) copy-start(f32[1024,512]{1,0:T(8,128)} %transform_ref.1) | copy-start | bytes 6291460
  6.2 8.0 %copy-start.2 = (bf16[4,128,1024]{2,1,0:T(8,128)(2,1)S(1)}, bf16[4,128,1024]{2,1,0:T(8,128)(2,1)}, u32[]{:S(2)}) copy-start(bf16[4,128,1024]{2,1,0:T(8,128)(2,1)} %param.6) | copy-start | bytes 3145732
  6.2 56.9 %all-to-all-start = ((bf16[8,64,4096]{2,1,0:T(8,128)(2,1)}), bf16[8,64,4096]{2,1,0:T(8,128)(2,1)}, u32[]{:S(2)}, u32[]{:S(2)}) async-start(bf16[8,64,4096]{2,1,0:T(8,128)(2,1)} %pick.1), calls=%async_computation | async-start | bytes 8388608 | tf_op jit(solution)/shard_map/all_to_all | solution.py:197
  63.0 6.0 %copy-start = (s16[4224,512]{1,0:T(8,128)(2,1)S(1)}, s16[4224,512]{1,0:T(8,128)(2,1)}, u32[]{:S(2)}) copy-start(s16[4224,512]{1,0:T(8,128)(2,1)} %all-gather.2) | copy-start | bytes 12976132
  68.1 5.3 %collective-permute-start = (f32[4,4,64,128]{3,2,1,0:T(8,128)S(1)}, f32[4,4,64,128]{3,2,1,0:T(8,128)S(1)}, u32[]{:S(2)}, u32[]{:S(2)}) collective-permute-start(f32[4,4,64,128]{3,2,1,0:T(8,128)S(1)} %contract.3), channel_id=1, source_target_pairs={{0,4},{4,0},{1,5},{5,1},{2,6},{6,2},{3,7},{7,3},{8,12},{12,8},{9,1... | collective-permute-start | bytes 1572872 | tf_op jit(solution)/shard_map/ppermute | solution.py:200

commit v5 on v4

--- a/solution.py
+++ b/solution.py
@@ -167,7 +167,7 @@
 def contract(amps, coded, core, ys, reps, grant):
     chunks, padded, cols = coded.shape
     groups, rows, depth = amps.shape
-    step = 2
+    step = 1
     shape = (ys, reps, rows, cols // reps)
     return pl.pallas_call(
         functools.partial(contract_kernel, step),

time: 91.9 us -> 92.8 us (level)
  no operation moved by 1% of the time
where the time goes in v5:
time: 92.8 us; the launch traced here: 92.3 us
  blocking collectives  64.1 us (69%)
  Pallas kernels  18.3 us (20%)
  starting transfers between devices  8.91 us (10%)
    all_gather x1, blocking collectives, body(): line = lax.all_gather(coded, 'z', axis=0, tiled=False)  46.7 us
    all_to_all x1, blocking collectives, body(): lax.all_to_all(partial, ('y', 'rep'), split_axis=0, concat_axis=0, tiled=...  17.4 us
    pallas_call x2, Pallas kernels, contract(): pl.pallas_call(functools.partial(contract_kernel, step), in_specs=[pl.Blo...  10.1 us
    all_to_all x1, starting transfers between devices, body(): lax.all_to_all(picked, ('y', 'core'), split_axis=0, concat_axis=0, tiled=...  7.94 us
    pallas_call x1, Pallas kernels, pick(): pl.pallas_call(functools.partial(pick_kernel, per_device, width), in_spec...  6.14 us
    pallas_call x1, Pallas kernels, fold(): pl.pallas_call(fold_kernel, out_shape=jax.ShapeDtypeStruct((rows + PAD, c...  2.08 us
  transfers between devices with their start and end apart: 2, of which 1 were waited for; matrix products, arithmetic and copies ran while one was open for 0% of the time, Pallas kernels for 7%

profile of v5, /device:TPU:1, one launch (start us, length us, event | category | flops | bytes accessed | tf_op | source)
XLA Modules:
  0.0 92.3 jit_solution(244309744655533646)
XLA Ops:
  0.0 6.1 %pick.1 = bf16[8,64,4096]{2,1,0:T(8,128)(2,1)} custom-call(s32[256]{0:T(256)} %sizes_ref.1, s32[1]{0:T(128)} %bitcast.1.rep_ref, bf16[64,65536]{1,0:T(8,128)(2,1)} %tau_hbm.1), custom_call_target="tpu_custom_call" | custom-call | bytes 12582912 | tf_op jit(solution)/shard_map/pick/pallas_call | solution.py:116
  6.2 0.0 copy-start.1
  6.2 0.0 copy-start.2
  6.2 7.9 %all-to-all-start = ((bf16[8,64,4096]{2,1,0:T(8,128)(2,1)}), bf16[8,64,4096]{2,1,0:T(8,128)(2,1)}, u32[]{:S(2)}, u32[]{:S(2)}) async-start(bf16[8,64,4096]{2,1,0:T(8,128)(2,1)} %pick.1), calls=%async_computation | async-start | bytes 8388608 | tf_op jit(solution)/shard_map/all_to_all | solution.py:197
  14.1 0.0 copy-done.1
  14.1 0.0 copy-done.2
  14.1 2.1 %fold.1 = s16[528,512]{1,0:T(8,128)(2,1)S(1)} custom-call(bf16[512,1024]{1,0:T(8,128)(2,1)S(1)} %bitcast.8, f32[1024,512]{1,0:T(8,128)S(1)} %copy-done.1), custom_call_target="tpu_custom_call" | custom-call | flops 1073741824 | bytes 4194304 | tf_op jit(solution)/shard_map/fold/pallas_call | solution.py:54
  16.2 46.7 %all-gather.2 = s16[4224,512]{1,0:T(8,128)(2,1)} all-gather(s16[528,512]{1,0:T(8,128)(2,1)S(1)} %fold.1), channel_id=2, replica_groups=mesh['z'=8,'y'=4,'core'=2,'rep'=4] {'z'}, dimensions={0}, use_global_device_ids=true | all-gather | bytes 4866048 | tf_op jit(solution)/shard_map/all_gather | solution.py:194
  62.9 0.1 all-to-all-done.amps_hbm
  63.0 0.0 copy-start
  63.1 5.5 %contract.3 = f32[4,4,64,128]{3,2,1,0:T(8,128)S(1)} custom-call(s32[1]{0:T(128)} %bitcast.4.core_ref, bf16[8,64,4096]{2,1,0:T(8,128)(2,1)} %all-to-all-done.amps_hbm, s16[8,528,512]{2,1,0:T(8,128)(2,1)} %bitcast.6), custom_call_target="tpu_custom_call" | custom-call | flops 2147483648 | bytes 7340032 | tf_op jit(solution)/shard_map/contract/pallas_call | solution.py:172
  68.5 1.0 %collective-permute-start = (f32[4,4,64,128]{3,2,1,0:T(8,128)S(1)}, f32[4,4,64,128]{3,2,1,0:T(8,128)S(1)}, u32[]{:S(2)}, u32[]{:S(2)}) collective-permute-start(f32[4,4,64,128]{3,2,1,0:T(8,128)S(1)} %contract.3), channel_id=1, source_target_pairs={{0,4},{4,0},{1,5},{5,1},{2,6},{6,2},{3,7},{7,3},{8,12},{12,8},{9,1... | collective-permute-start | bytes 1572872 | tf_op jit(solution)/shard_map/ppermute | solution.py:200
  69.5 0.0 copy-done
  69.5 4.7 %contract.2 = f32[4,4,64,128]{3,2,1,0:T(8,128)S(1)} custom-call(s32[1]{0:T(128)} %bitcast.core_ref, bf16[8,64,4096]{2,1,0:T(8,128)(2,1)} %all-to-all-done.amps_hbm, s16[8,528,512]{2,1,0:T(8,128)(2,1)S(1)} %bitcast.7), custom_call_target="tpu_custom_call" | custom-call | flops 2147483648 | bytes 7340032 | tf_op jit(solution)/shard_map/contract/pallas_call | solution.py:172
  74.2 0.0 collective-permute-done
  74.2 0.1 add.3
  74.2 17.4 %all_to_all.10 = f32[16,64,128]{2,1,0:T(8,128)S(1)} all-to-all(f32[16,64,128]{2,1,0:T(8,128)S(1)} %bitcast.9), channel_id=1, replica_groups=mesh['z'=8,'y'=4,'core'=2,'rep'=4] {'y','rep'}, dimensions={0} | all-to-all | bytes 1048576 | tf_op jit(solution)/shard_map/all_to_all | solution.py:203
  91.7 0.6 reduce_sum.9
Async XLA Ops:
  6.2 8.0 %copy-start.1 = (f32[1024,512]{1,0:T(8,128)S(1)}, f32[1024,512]{1,0:T(8,128)}, u32[]{:S(2)}) copy-start(f32[1024,512]{1,0:T(8,128)} %transform_ref.1) | copy-start | bytes 6291460
  6.2 8.0 %copy-start.2 = (bf16[4,128,1024]{2,1,0:T(8,128)(2,1)S(1)}, bf16[4,128,1024]{2,1,0:T(8,128)(2,1)}, u32[]{:S(2)}) copy-start(bf16[4,128,1024]{2,1,0:T(8,128)(2,1)} %param.6) | copy-start | bytes 3145732
  6.2 56.9 %all-to-all-start = ((bf16[8,64,4096]{2,1,0:T(8,128)(2,1)}), bf16[8,64,4096]{2,1,0:T(8,128)(2,1)}, u32[]{:S(2)}, u32[]{:S(2)}) async-start(bf16[8,64,4096]{2,1,0:T(8,128)(2,1)} %pick.1), calls=%async_computation | async-start | bytes 8388608 | tf_op jit(solution)/shard_map/all_to_all | solution.py:197
  63.0 6.4 %copy-start = (s16[4224,512]{1,0:T(8,128)(2,1)S(1)}, s16[4224,512]{1,0:T(8,128)(2,1)}, u32[]{:S(2)}) copy-start(s16[4224,512]{1,0:T(8,128)(2,1)} %all-gather.2) | copy-start | bytes 12976132
  68.5 5.6 %collective-permute-start = (f32[4,4,64,128]{3,2,1,0:T(8,128)S(1)}, f32[4,4,64,128]{3,2,1,0:T(8,128)S(1)}, u32[]{:S(2)}, u32[]{:S(2)}) collective-permute-start(f32[4,4,64,128]{3,2,1,0:T(8,128)S(1)} %contract.3), channel_id=1, source_target_pairs={{0,4},{4,0},{1,5},{5,1},{2,6},{6,2},{3,7},{7,3},{8,12},{12,8},{9,1... | collective-permute-start | bytes 1572872 | tf_op jit(solution)/shard_map/ppermute | solution.py:200
